TPU v7x, 512 devices: a whole 4x4x16 slice. The times are simulated.
512 devices in a mesh: grp: 8 (over y, core), mem: 64 (over x, z).
Axes of the slice: x: 4, y: 4, z: 16, core: 2. Of those that a mesh axis runs over, the one named last changes fastest.
Arguments:
- tokens: bfloat16 [65536, 1024], P(('grp', 'mem')), may hold values from -6 to 6
- cotangent: bfloat16 [65536, 1024], P(('grp', 'mem')), may hold values from -6 to 6
- path: int32 [512, 3], P(('grp', 'mem')), may hold values from 0 to 1023, as said below
- coarse_weights: bfloat16 [4, 1024, 512], P(None, 'mem'), may hold values from -0.1875 to 0.1875
- middle_weights: bfloat16 [64, 1024, 256], P(None, 'mem'), may hold values from -0.1875 to 0.1875
- fine_weights: bfloat16 [1024, 1024, 128], P('grp', 'mem'), may hold values from -0.1875 to 0.1875
Outputs:
- tokens_grad: bfloat16 [65536, 1024], P(('grp', 'mem'))
- coarse_grad: bfloat16 [4, 1024, 512], P(None, 'mem')
- middle_grad: bfloat16 [64, 1024, 256], P(None, 'mem')
- fine_grad: bfloat16 [1024, 1024, 128], P('grp', 'mem')
Inputs may be any that keep to these rules, and one draw needn't show every extreme that they name: Row d is the path of document d: column 0 its coarse block, column 1 its middle block, column 2 its fine block, with middle = fine * 64 // 1024 and coarse = middle * 4 // 64. Some fine blocks are chosen by many documents.
All inputs are finite; a program needn't handle non-finite values.
Results may differ from a plain program's by a relative error of at most 0.005.
Values may be sent and summed in bfloat16 or wider, within the bound.
No kernel may reach another device: no remote copies, remote signals or barrier semaphores. Data moves between devices by JAX's collectives and lax.ppermute only.
A program may use at most 64 MiB of HBM per device.

v0:
```python
from functools import partial
import jax
import jax.numpy as jnp
from jax import lax
from jax.sharding import PartitionSpec as P


def contract_rows(left, right):
    return lax.dot_general(
        left, right, (((0,), (0,)), ((), ())), preferred_element_type=jnp.float32
    )


def level_terms(inputs, upstream, weights):
    hidden_width = weights.shape[1] // 2
    up_half = weights[:, :hidden_width]
    down_half = weights[:, hidden_width:]
    before = jnp.dot(inputs, up_half, preferred_element_type=jnp.float32)
    hidden, pullback = jax.vjp(partial(jax.nn.gelu, approximate=True), before)
    hidden_low = hidden.astype(jnp.bfloat16)
    hidden_grad = jnp.dot(upstream, down_half, preferred_element_type=jnp.float32)
    before_grad = pullback(hidden_grad)[0].astype(jnp.bfloat16)
    up_grad = contract_rows(inputs, before_grad)
    down_grad = contract_rows(upstream, hidden_low)
    input_part = lax.dot_general(
        before_grad, up_half, (((1,), (1,)), ((), ())), preferred_element_type=jnp.float32
    )
    return (jnp.concatenate([up_grad, down_grad], axis=1), input_part)


def one_hot_rows(identity, count):
    return (identity[:, None] == jnp.arange(count, dtype=jnp.int32)[None, :]).astype(jnp.bfloat16)


def select_blocks(picker, blocks):
    return jnp.einsum("mk,krh->mrh", picker, blocks, preferred_element_type=jnp.float32).astype(
        jnp.bfloat16
    )


def collect_blocks(picker, pieces):
    return jnp.einsum(
        "mk,mrh->krh", picker.astype(jnp.float32), pieces, precision=lax.Precision.HIGHEST
    )


def on_device(tokens, cotangent, path, coarse_weights, middle_weights, fine_weights):
    member_count = lax.axis_size("mem")
    group_count = lax.axis_size("grp")
    group = lax.axis_index("grp")
    row_count = coarse_weights.shape[1]
    fine_owned = fine_weights.shape[0]
    route = path[0]
    all_paths = lax.all_gather(path, ("grp", "mem"), axis=0, tiled=True)
    group_paths = lax.dynamic_slice_in_dim(all_paths, group * member_count, member_count, 0)
    coarse_pick = one_hot_rows(group_paths[:, 0], coarse_weights.shape[0])
    middle_pick = one_hot_rows(group_paths[:, 1], middle_weights.shape[0])
    middle_send = select_blocks(middle_pick, middle_weights)
    every_block = lax.all_gather(coarse_weights, "mem", axis=1, tiled=True)
    coarse_block = lax.dynamic_index_in_dim(every_block, route[0], 0, keepdims=False)
    middle_block = lax.all_to_all(middle_send, "mem", split_axis=0, concat_axis=1, tiled=True)[0]
    offsets = all_paths[:, 2] - group * fine_owned
    fine_pick = one_hot_rows(offsets, fine_owned)
    fine_send = select_blocks(fine_pick, fine_weights).reshape(
        group_count, member_count, row_count, fine_weights.shape[2]
    )
    arrived = lax.all_to_all(fine_send, "grp", split_axis=0, concat_axis=0, tiled=True)
    merged = jnp.sum(arrived, axis=0, dtype=jnp.float32).astype(jnp.bfloat16)
    fine_block = lax.all_to_all(merged, "mem", split_axis=0, concat_axis=1, tiled=True)[0]
    coarse_term, coarse_back = level_terms(tokens, cotangent, coarse_block)
    middle_term, middle_back = level_terms(tokens, cotangent, middle_block)
    fine_term, fine_back = level_terms(tokens, cotangent, fine_block)
    tokens_grad = (coarse_back + middle_back + fine_back).astype(jnp.bfloat16)
    coarse_parts, middle_parts = (
        lax.all_to_all(
            coarse_term.reshape(member_count, row_count, -1),
            "mem",
            split_axis=0,
            concat_axis=0,
            tiled=True,
        ),
        lax.all_to_all(
            middle_term.reshape(member_count, row_count, -1),
            "mem",
            split_axis=0,
            concat_axis=0,
            tiled=True,
        ),
    )
    coarse_local = collect_blocks(coarse_pick, coarse_parts)
    middle_local = collect_blocks(middle_pick, middle_parts)
    coarse_total, middle_total = lax.psum((coarse_local, middle_local), "grp")
    fine_parts = lax.all_to_all(
        fine_term.reshape(member_count, row_count, -1),
        "mem",
        split_axis=0,
        concat_axis=0,
        tiled=True,
    )
    owner_group = group_paths[:, 2] // fine_owned
    destined = (jnp.arange(group_count, dtype=jnp.int32)[:, None] == owner_group[None, :]).astype(
        jnp.float32
    )
    outgoing = destined[:, :, None, None] * fine_parts[None]
    returned = lax.all_to_all(outgoing, "grp", split_axis=0, concat_axis=0, tiled=True)
    fine_local = collect_blocks(
        fine_pick, returned.reshape(group_count * member_count, row_count, -1)
    )
    return (
        tokens_grad,
        coarse_total.astype(jnp.bfloat16),
        middle_total.astype(jnp.bfloat16),
        fine_local.astype(jnp.bfloat16),
    )


def solution(mesh):
    return jax.shard_map(
        on_device,
        mesh=mesh,
        in_specs=(
            P(("grp", "mem"), None),
            P(("grp", "mem"), None),
            P(("grp", "mem"), None),
            P(None, "mem", None),
            P(None, "mem", None),
            P("grp", "mem", None),
        ),
        out_specs=(
            P(("grp", "mem"), None),
            P(None, "mem", None),
            P(None, "mem", None),
            P("grp", "mem", None),
        ),
        check_vma=False,
    )
```

profile of v0, /device:TPU:63, one launch (start us, length us, event | category | flops | bytes accessed | tf_op | source)
XLA Modules:
  0.0 555.5 jit_solution(7141725121758117286)
XLA Ops:
  7.2 104.7 %all-gather = s32[512,1,3]{2,1,0:T(1,128)S(1)} all-gather(s32[1,1,3]{2,1,0:T(1,128)} %bitcast.100), channel_id=1, replica_groups=mesh['grp'=8,'mem'=64] {'grp','mem'}, dimensions={0}, use_global_device_ids=true | all-gather | bytes 6156 | tf_op jit(solution)/shard_map/all_gather | solution.py:54
  113.2 32.7 %all_to_all.43 = bf16[8,64,16,128]{3,1,2,0:T(8,128)(2,1)S(1)} all-to-all(bf16[8,64,16,128]{3,1,2,0:T(8,128)(2,1)S(1)} %copy.78), channel_id=1, replica_groups=mesh['grp'=8,'mem'=64] {'grp'}, dimensions={0} | all-to-all | bytes 4194304 | tf_op jit(solution)/shard_map/all_to_all | solution.py:67
  146.2 0.9 copy.80
  147.1 12.7 %all-to-all-start.2 = ((bf16[64,16,128]{2,1,0:T(8,128)(2,1)}), bf16[64,16,128]{2,1,0:T(8,128)(2,1)S(1)}, u32[]{:S(2)}, u32[]{:S(2)}) async-start(bf16[64,16,128]{2,1,0:T(8,128)(2,1)} %copy.80), calls=%async_computation.2 | async-start | bytes 524288 | tf_op jit(solution)/shard_map/all_to_all | solution.py:69
  159.9 1.4 convolution_convert_fusion.1
  161.3 1.1 copy.75
  162.4 16.9 %all-to-all-done.2 = bf16[64,16,128]{2,1,0:T(8,128)(2,1)S(1)} async-done(((bf16[64,16,128]{2,1,0:T(8,128)(2,1)}), bf16[64,16,128]{2,1,0:T(8,128)(2,1)S(1)}, u32[]{:S(2)}, u32[]{:S(2)}) %all-to-all-start.2) | async-done | bytes 262176 | tf_op jit(solution)/shard_map/all_to_all | solution.py:69
  179.3 7.3 %all-to-all-start = ((bf16[64,16,256]{2,1,0:T(8,128)(2,1)}), bf16[64,16,256]{2,1,0:T(8,128)(2,1)S(1)}, u32[]{:S(2)}, u32[]{:S(2)}) async-start(bf16[64,16,256]{2,1,0:T(8,128)(2,1)} %copy.75), calls=%async_computation | async-start | bytes 1048576 | tf_op jit(solution)/shard_map/all_to_all | solution.py:61
  187.6 1.0 copy.85
  188.6 28.1 %all-to-all-done = bf16[64,16,256]{2,1,0:T(8,128)(2,1)S(1)} async-done(((bf16[64,16,256]{2,1,0:T(8,128)(2,1)}), bf16[64,16,256]{2,1,0:T(8,128)(2,1)S(1)}, u32[]{:S(2)}, u32[]{:S(2)}) %all-to-all-start) | async-done | bytes 524320 | tf_op jit(solution)/shard_map/all_to_all | solution.py:61
  216.7 8.0 %all-to-all-start.5 = ((f32[64,16,128]{2,1,0:T(8,128)}), f32[64,16,128]{2,1,0:T(8,128)}, u32[]{:S(2)}, u32[]{:S(2)}) async-start(f32[64,16,128]{2,1,0:T(8,128)} %bitcast.30), calls=%async_computation.5 | async-start | bytes 1048576 | tf_op jit(solution)/shard_map/all_to_all | solution.py:93
  226.6 1.3 copy.83
  228.0 28.1 %all-to-all-done.5 = f32[64,16,128]{2,1,0:T(8,128)} async-done(((f32[64,16,128]{2,1,0:T(8,128)}), f32[64,16,128]{2,1,0:T(8,128)}, u32[]{:S(2)}, u32[]{:S(2)}) %all-to-all-start.5) | async-done | bytes 524320 | tf_op jit(solution)/shard_map/all_to_all | solution.py:93
  256.0 6.6 %all-to-all-start.4 = ((f32[64,16,256]{2,1,0:T(8,128)}), f32[64,16,256]{2,1,0:T(8,128)S(1)}, u32[]{:S(2)}, u32[]{:S(2)}) async-start(f32[64,16,256]{2,1,0:T(8,128)} %bitcast.25), calls=%async_computation.4 | async-start | bytes 2097152 | tf_op jit(solution)/shard_map/all_to_all | solution.py:82
  262.7 1.2 copy.86
  263.9 2.6 broadcast_multiply_fusion
  266.5 51.7 %all-to-all-done.4 = f32[64,16,256]{2,1,0:T(8,128)S(1)} async-done(((f32[64,16,256]{2,1,0:T(8,128)}), f32[64,16,256]{2,1,0:T(8,128)S(1)}, u32[]{:S(2)}, u32[]{:S(2)}) %all-to-all-start.4) | async-done | bytes 1048608 | tf_op jit(solution)/shard_map/all_to_all | solution.py:82
  318.2 1.0 copy-done.2
  319.2 9.0 %all-to-all-start.6 = ((f32[8,64,16,128]{3,1,2,0:T(8,128)}), f32[8,64,16,128]{3,1,2,0:T(8,128)}, u32[]{:S(2)}, u32[]{:S(2)}) async-start(f32[8,64,16,128]{3,1,2,0:T(8,128)} %broadcast_multiply_fusion), calls=%async_computation.6 | async-start | bytes 8388608 | tf_op jit(solution)/shard_map/all_to_all | solution.py:105
  328.4 50.9 %all-gather.3.cloned.1.call-done = bf16[4,1024,512]{2,1,0:T(8,128)(2,1)} async-done(((bf16[4,16,512]{2,1,0:T(8,128)(2,1)}), bf16[4,1024,512]{2,1,0:T(8,128)(2,1)}) %all-gather.3.cloned.1.call-update) | async-done | bytes 4194320 | tf_op jit(solution)/shard_map/all_gather | solution.py:59
  379.3 1.3 dynamic-slice_bitcast_fusion
  382.0 1.9 copy.81
  383.9 10.2 %all-to-all-start.3 = ((f32[64,16,512]{2,1,0:T(8,128)}), f32[64,16,512]{2,1,0:T(8,128)S(1)}, u32[]{:S(2)}, u32[]{:S(2)}) async-start(f32[64,16,512]{2,1,0:T(8,128)} %bitcast.89), calls=%async_computation.3 | async-start | bytes 4194304 | tf_op jit(solution)/shard_map/all_to_all | solution.py:75
  394.1 3.6 fusion.3
  398.3 1.0 fusion.2
  399.3 2.5 copy.87
  401.8 1.7 convolution_convert_fusion.2
  403.5 1.1 copy.90
  404.6 81.4 %all-to-all-done.3 = f32[64,16,512]{2,1,0:T(8,128)S(1)} async-done(((f32[64,16,512]{2,1,0:T(8,128)}), f32[64,16,512]{2,1,0:T(8,128)S(1)}, u32[]{:S(2)}, u32[]{:S(2)}) %all-to-all-start.3) | async-done | bytes 2097184 | tf_op jit(solution)/shard_map/all_to_all | solution.py:75
  486.0 2.0 fusion
  488.0 59.0 %all-reduce.2 = (bf16[4,16,512]{2,0,1:T(4,128)(2,1)S(1)}, bf16[64,16,256]{2,0,1:T(8,128)(2,1)S(1)}) all-reduce(f32[4,16,512]{2,0,1:T(4,128)S(1)} %fusion, f32[64,16,256]{2,0,1:T(8,128)} %fusion.3), channel_id=1, replica_groups=mesh['grp'=8,'mem'=64] {'grp'}, use_global_device_ids=true, to_apply=%region_1.2 | all-reduce | flops 294912 | bytes 1769472 | tf_op jit(solution)/shard_map/psum | solution.py:92
  547.6 1.1 copy.89
  (47 shorter events, 7.1 us)
Async XLA Ops:
  7.2 105.0 %copy-start = (bf16[128,16,128]{2,1,0:T(8,128)(2,1)S(1)}, bf16[128,16,128]{2,1,0:T(8,128)(2,1)}, u32[]{:S(2)}) copy-start(bf16[128,16,128]{2,1,0:T(8,128)(2,1)} %param.11) | copy-start | bytes 1572868
  146.2 40.4 %copy-start.1 = (bf16[128,1024]{1,0:T(8,128)(2,1)S(1)}, bf16[128,1024]{1,0:T(8,128)(2,1)}, u32[]{:S(2)}) copy-start(bf16[128,1024]{1,0:T(8,128)(2,1)} %param.6) | copy-start | bytes 786436
  147.1 39.8 %copy-start.5 = (bf16[128,1024]{1,0:T(8,128)(2,1)S(1)}, bf16[128,1024]{1,0:T(8,128)(2,1)}, u32[]{:S(2)}) copy-start(bf16[128,1024]{1,0:T(8,128)(2,1)} %param.7) | copy-start | bytes 786436
  147.1 32.2 %all-to-all-start.2 = ((bf16[64,16,128]{2,1,0:T(8,128)(2,1)}), bf16[64,16,128]{2,1,0:T(8,128)(2,1)S(1)}, u32[]{:S(2)}, u32[]{:S(2)}) async-start(bf16[64,16,128]{2,1,0:T(8,128)(2,1)} %copy.80), calls=%async_computation.2 | async-start | bytes 524288 | tf_op jit(solution)/shard_map/all_to_all | solution.py:69
  179.3 37.4 %all-to-all-start = ((bf16[64,16,256]{2,1,0:T(8,128)(2,1)}), bf16[64,16,256]{2,1,0:T(8,128)(2,1)S(1)}, u32[]{:S(2)}, u32[]{:S(2)}) async-start(bf16[64,16,256]{2,1,0:T(8,128)(2,1)} %copy.75), calls=%async_computation | async-start | bytes 1048576 | tf_op jit(solution)/shard_map/all_to_all | solution.py:61
  216.7 9.8 %copy-start.6 = (bf16[64,16,256]{2,1,0:T(8,128)(2,1)}, bf16[64,16,256]{2,1,0:T(8,128)(2,1)S(1)}, u32[]{:S(2)}) copy-start(bf16[64,16,256]{2,1,0:T(8,128)(2,1)S(1)} %all-to-all-done) | copy-start | bytes 1572868
  216.7 39.3 %all-to-all-start.5 = ((f32[64,16,128]{2,1,0:T(8,128)}), f32[64,16,128]{2,1,0:T(8,128)}, u32[]{:S(2)}, u32[]{:S(2)}) async-start(f32[64,16,128]{2,1,0:T(8,128)} %bitcast.30), calls=%async_computation.5 | async-start | bytes 1048576 | tf_op jit(solution)/shard_map/all_to_all | solution.py:93
  224.8 154.5 %all-gather.3.cloned.1.call-start = ((), (), s32[]{:S(2)}) async-start(), calls=%async_computation.7 | async-start | bytes 4259840 | tf_op jit(solution)/shard_map/all_gather | solution.py:59
  256.0 62.2 %all-to-all-start.4 = ((f32[64,16,256]{2,1,0:T(8,128)}), f32[64,16,256]{2,1,0:T(8,128)S(1)}, u32[]{:S(2)}, u32[]{:S(2)}) async-start(f32[64,16,256]{2,1,0:T(8,128)} %bitcast.25), calls=%async_computation.4 | async-start | bytes 2097152 | tf_op jit(solution)/shard_map/all_to_all | solution.py:82
  266.5 61.8 %copy-start.8 = (s32[1,3]{1,0:T(1,128)S(1)}, s32[1,3]{1,0:T(1,128)}, u32[]{:S(2)}) copy-start(s32[1,3]{1,0:T(1,128)} %param.8) | copy-start | bytes 40
  318.2 1.0 copy-start.2
  319.2 64.7 %all-to-all-start.6 = ((f32[8,64,16,128]{3,1,2,0:T(8,128)}), f32[8,64,16,128]{3,1,2,0:T(8,128)}, u32[]{:S(2)}, u32[]{:S(2)}) async-start(f32[8,64,16,128]{3,1,2,0:T(8,128)} %broadcast_multiply_fusion), calls=%async_computation.6 | async-start | bytes 8388608 | tf_op jit(solution)/shard_map/all_to_all | solution.py:105
  380.6 1.0 copy-start.3
  383.9 102.1 %all-to-all-start.3 = ((f32[64,16,512]{2,1,0:T(8,128)}), f32[64,16,512]{2,1,0:T(8,128)S(1)}, u32[]{:S(2)}, u32[]{:S(2)}) async-start(f32[64,16,512]{2,1,0:T(8,128)} %bitcast.89), calls=%async_computation.3 | async-start | bytes 4194304 | tf_op jit(solution)/shard_map/all_to_all | solution.py:75
  394.1 3.6 copy-start.4
  394.1 4.0 copy-start.7
Sparse Core Ops, SparseCore 0:
  228.6 150.6 all-gather.2
where the time goes:
time: 556 us
  waiting for transfers between devices  258 us (46%)
  blocking collectives  196 us (35%)
  starting transfers between devices  53.9 us (10%)
  local copies, waits for them, and re-layouts  15.4 us (3%)
  between operations  14.5 us (3%)
  matrix products  14.1 us (3%)
    all_gather x1, blocking collectives, on_device(): all_paths = lax.all_gather(path, ('grp', 'mem'), axis=0, tiled=True)  105 us
    all_to_all x1, waiting for transfers between devices, on_device(): lax.all_to_all(coarse_term.reshape(member_count, row_count, -1), 'mem', s...  81.4 us
    psum x1, blocking collectives, on_device(): coarse_total, middle_total = lax.psum((coarse_local, middle_local), 'grp')  59 us
    all_to_all x1, waiting for transfers between devices, on_device(): lax.all_to_all(middle_term.reshape(member_count, row_count, -1), 'mem', s...  51.7 us
    all_gather x1, waiting for transfers between devices, on_device(): every_block = lax.all_gather(coarse_weights, 'mem', axis=1, tiled=True)  50.9 us
    all_to_all x1, blocking collectives, on_device(): lax.all_to_all(fine_send, 'grp', split_axis=0, concat_axis=0, tiled=True)  32.7 us
    all_to_all x1, waiting for transfers between devices, on_device(): lax.all_to_all(middle_send, 'mem', split_axis=0, concat_axis=1, tiled=True)  28.1 us
    all_to_all x1, waiting for transfers between devices, on_device(): lax.all_to_all(fine_term.reshape(member_count, row_count, -1), 'mem', spl...  28.1 us
  transfers between devices with their start and end apart: 7, of which 6 were waited for; matrix products, arithmetic and copies ran while one was open for 5% of the time, Pallas kernels for 0%

commit v1 on v0

--- a/solution.py
+++ b/solution.py
@@ -3,6 +3,18 @@
 import jax.numpy as jnp
 from jax import lax
 from jax.sharding import PartitionSpec as P
+
+
+def in_blocks(x, dim, count):
+    shape = x.shape
+    pieces = x.reshape(*shape[:dim], count, shape[dim] // count, *shape[dim + 1 :])
+    return jnp.moveaxis(pieces, dim, 0)
+
+
+def in_order(tiles, dim):
+    shape = list(tiles.shape[1:])
+    shape[dim] *= tiles.shape[0]
+    return jnp.moveaxis(tiles, 0, dim).reshape(shape)
 
 
 def contract_rows(left, right):
@@ -102,7 +114,14 @@
         jnp.float32
     )
     outgoing = destined[:, :, None, None] * fine_parts[None]
-    returned = lax.all_to_all(outgoing, "grp", split_axis=0, concat_axis=0, tiled=True)
+    devices, mine = (lax.axis_size("grp"), lax.axis_index("grp"))
+    blocks_2 = in_blocks(outgoing, 0, devices)
+    outs = [blocks_2[mine]]
+    for turn in range(1, devices):
+        sent = blocks_2[mine ^ turn]
+        outs.append(lax.ppermute(sent, "grp", [(i, i ^ turn) for i in range(devices)]))
+    blocks_2 = jnp.stack(outs)[mine ^ jnp.arange(devices)]
+    returned = in_order(blocks_2, 0)
     fine_local = collect_blocks(
         fine_pick, returned.reshape(group_count * member_count, row_count, -1)
     )

time: 556 us -> 499 us (0.90)
  the two profiles are of different devices: /device:TPU:63 before, /device:TPU:31 now
where the time goes in v1:
time: 499 us; the launch traced here: 498 us
  waiting for transfers between devices  185 us (37%)
  blocking collectives  165 us (33%)
  starting transfers between devices  82.4 us (17%)
  local copies, waits for them, and re-layouts  31.2 us (6%)
  matrix products  17.2 us (3%)
  between operations  14.6 us (3%)
    all_gather x1, blocking collectives, on_device(): all_paths = lax.all_gather(path, ('grp', 'mem'), axis=0, tiled=True)  105 us
    psum x1, blocking collectives, on_device(): coarse_total, middle_total = lax.psum((coarse_local, middle_local), 'grp')  59.9 us
    ppermute x7, waiting for transfers between devices, on_device(): lax.ppermute(sent, 'grp', [(i, i ^ turn) for i in range(devices)])  37.2 us
    all_to_all x1, waiting for transfers between devices, on_device(): lax.all_to_all(fine_term.reshape(member_count, row_count, -1), 'mem', spl...  33.1 us
    all_to_all x1, waiting for transfers between devices, on_device(): lax.all_to_all(middle_term.reshape(member_count, row_count, -1), 'mem', s...  29.7 us
    all_to_all x1, waiting for transfers between devices, on_device(): lax.all_to_all(middle_send, 'mem', split_axis=0, concat_axis=1, tiled=True)  26.7 us
    all_to_all x1, waiting for transfers between devices, on_device(): lax.all_to_all(fine_send, 'grp', split_axis=0, concat_axis=0, tiled=True)  23.9 us
    ppermute x7, starting transfers between devices, on_device(): lax.ppermute(sent, 'grp', [(i, i ^ turn) for i in range(devices)])  23 us
  transfers between devices with their start and end apart: 14, of which 11 were waited for; matrix products, arithmetic and copies ran while one was open for 9% of the time, Pallas kernels for 0%

profile of v1, /device:TPU:31, one launch (start us, length us, event | category | flops | bytes accessed | tf_op | source)
XLA Modules:
  0.0 497.9 jit_solution(6152741524792309962)
XLA Ops:
  7.2 105.3 %all-gather = s32[512,1,3]{2,1,0:T(1,128)S(1)} all-gather(s32[1,1,3]{2,1,0:T(1,128)} %bitcast.130), channel_id=1, replica_groups=mesh['grp'=8,'mem'=64] {'grp','mem'}, dimensions={0}, use_global_device_ids=true | all-gather | bytes 6156 | tf_op jit(solution)/shard_map/all_gather | solution.py:66
  115.0 10.4 %all-to-all-start.1 = ((bf16[8,64,16,128]{3,1,2,0:T(8,128)(2,1)}), bf16[8,64,16,128]{3,1,2,0:T(8,128)(2,1)S(1)}, u32[]{:S(2)}, u32[]{:S(2)}) async-start(bf16[8,64,16,128]{3,1,2,0:T(8,128)(2,1)} %copy.94), calls=%async_computation.1 | async-start | bytes 4194304 | tf_op jit(solution)/shard_map/all_to_all | solution.py:79
  126.1 23.9 %all-to-all-done.1 = bf16[8,64,16,128]{3,1,2,0:T(8,128)(2,1)S(1)} async-done(((bf16[8,64,16,128]{3,1,2,0:T(8,128)(2,1)}), bf16[8,64,16,128]{3,1,2,0:T(8,128)(2,1)S(1)}, u32[]{:S(2)}, u32[]{:S(2)}) %all-to-all-start.1) | async-done | bytes 2097184 | tf_op jit(solution)/shard_map/all_to_all | solution.py:79
  151.3 11.2 %all-to-all-start.2 = ((bf16[64,16,128]{2,1,0:T(8,128)(2,1)}), bf16[64,16,128]{2,1,0:T(8,128)(2,1)S(1)}, u32[]{:S(2)}, u32[]{:S(2)}) async-start(bf16[64,16,128]{2,1,0:T(8,128)(2,1)} %copy.96), calls=%async_computation.2 | async-start | bytes 524288 | tf_op jit(solution)/shard_map/all_to_all | solution.py:81
  165.8 16.3 %all-to-all-done.2 = bf16[64,16,128]{2,1,0:T(8,128)(2,1)S(1)} async-done(((bf16[64,16,128]{2,1,0:T(8,128)(2,1)}), bf16[64,16,128]{2,1,0:T(8,128)(2,1)S(1)}, u32[]{:S(2)}, u32[]{:S(2)}) %all-to-all-start.2) | async-done | bytes 262176 | tf_op jit(solution)/shard_map/all_to_all | solution.py:81
  182.1 8.4 %all-to-all-start = ((bf16[64,16,256]{2,1,0:T(8,128)(2,1)}), bf16[64,16,256]{2,1,0:T(8,128)(2,1)S(1)}, u32[]{:S(2)}, u32[]{:S(2)}) async-start(bf16[64,16,256]{2,1,0:T(8,128)(2,1)} %copy.91), calls=%async_computation | async-start | bytes 1048576 | tf_op jit(solution)/shard_map/all_to_all | solution.py:73
  192.5 26.7 %all-to-all-done = bf16[64,16,256]{2,1,0:T(8,128)(2,1)S(1)} async-done(((bf16[64,16,256]{2,1,0:T(8,128)(2,1)}), bf16[64,16,256]{2,1,0:T(8,128)(2,1)S(1)}, u32[]{:S(2)}, u32[]{:S(2)}) %all-to-all-start) | async-done | bytes 524320 | tf_op jit(solution)/shard_map/all_to_all | solution.py:73
  219.1 9.7 %all-to-all-start.5 = ((f32[64,16,128]{2,1,0:T(8,128)}), f32[64,16,128]{2,1,0:T(8,128)}, u32[]{:S(2)}, u32[]{:S(2)}) async-start(f32[64,16,128]{2,1,0:T(8,128)} %bitcast.30), calls=%async_computation.5 | async-start | bytes 1048576 | tf_op jit(solution)/shard_map/all_to_all | solution.py:105
  231.3 33.1 %all-to-all-done.5 = f32[64,16,128]{2,1,0:T(8,128)} async-done(((f32[64,16,128]{2,1,0:T(8,128)}), f32[64,16,128]{2,1,0:T(8,128)}, u32[]{:S(2)}, u32[]{:S(2)}) %all-to-all-start.5) | async-done | bytes 524320 | tf_op jit(solution)/shard_map/all_to_all | solution.py:105
  264.4 7.9 %all-to-all-start.4 = ((f32[64,16,256]{2,1,0:T(8,128)}), f32[64,16,256]{2,1,0:T(8,128)}, u32[]{:S(2)}, u32[]{:S(2)}) async-start(f32[64,16,256]{2,1,0:T(8,128)} %bitcast.25), calls=%async_computation.4 | async-start | bytes 2097152 | tf_op jit(solution)/shard_map/all_to_all | solution.py:94
  272.4 17.2 %all-gather.3.cloned.1.call-done = bf16[4,1024,512]{2,1,0:T(8,128)(2,1)} async-done(((bf16[4,16,512]{2,1,0:T(8,128)(2,1)}), bf16[4,1024,512]{2,1,0:T(8,128)(2,1)}) %all-gather.3.cloned.1.call-update) | async-done | bytes 4194320 | tf_op jit(solution)/shard_map/all_gather | solution.py:71
  292.3 1.9 copy.97
  294.2 29.7 %all-to-all-done.4 = f32[64,16,256]{2,1,0:T(8,128)} async-done(((f32[64,16,256]{2,1,0:T(8,128)}), f32[64,16,256]{2,1,0:T(8,128)}, u32[]{:S(2)}, u32[]{:S(2)}) %all-to-all-start.4) | async-done | bytes 1048608 | tf_op jit(solution)/shard_map/all_to_all | solution.py:94
  323.9 11.9 %all-to-all-start.3 = ((f32[64,16,512]{2,1,0:T(8,128)}), f32[64,16,512]{2,1,0:T(8,128)S(1)}, u32[]{:S(2)}, u32[]{:S(2)}) async-start(f32[64,16,512]{2,1,0:T(8,128)} %bitcast.119), calls=%async_computation.3 | async-start | bytes 4194304 | tf_op jit(solution)/shard_map/all_to_all | solution.py:87
  337.5 1.9 copy-done.1
  341.1 3.7 collective-permute-start
  344.8 2.4 collective-permute-start.1
  347.3 3.0 collective-permute-start.2
  352.2 4.1 collective-permute-start.3
  356.3 3.1 collective-permute-start.4
  359.4 3.0 collective-permute-start.5
  364.3 3.6 collective-permute-start.6
  369.9 2.7 collective-permute-done.2
  373.4 10.5 %collective-permute-done.3 = f32[1,64,16,128]{3,2,1,0:T(8,128)S(1)} collective-permute-done((f32[1,64,16,128]{3,2,1,0:T(8,128)}, f32[1,64,16,128]{3,2,1,0:T(8,128)S(1)}, u32[]{:S(2)}, u32[]{:S(2)}) %collective-permute-start.3) | collective-permute-done | bytes 524320 | tf_op jit(solution)/shard_map/ppermute | solution.py:122
  384.7 10.8 %collective-permute-done.4 = f32[1,64,16,128]{3,2,1,0:T(8,128)S(1)} collective-permute-done((f32[1,64,16,128]{3,2,1,0:T(8,128)}, f32[1,64,16,128]{3,2,1,0:T(8,128)S(1)}, u32[]{:S(2)}, u32[]{:S(2)}) %collective-permute-start.4) | collective-permute-done | bytes 524320 | tf_op jit(solution)/shard_map/ppermute | solution.py:122
  396.3 2.4 collective-permute-done.5
  399.6 10.8 %collective-permute-done.6 = f32[1,64,16,128]{3,2,1,0:T(8,128)S(1)} collective-permute-done((f32[1,64,16,128]{3,2,1,0:T(8,128)S(1)}, f32[1,64,16,128]{3,2,1,0:T(8,128)S(1)}, u32[]{:S(2)}, u32[]{:S(2)}) %collective-permute-start.6) | collective-permute-done | bytes 524320 | tf_op jit(solution)/shard_map/ppermute | solution.py:122
  411.3 4.9 gather_fusion
  416.2 5.0 %fusion.4 = bf16[128,16,128]{2,0,1:T(8,128)(2,1)S(1)} fusion(f32[512,16,128]{2,1,0:T(8,128)} %bitcast.118, s32[512]{0:T(512)S(1)} %fusion.17), kind=kOutput, calls=%fused_computation.11 | convolution fusion | flops 1610940416 | bytes 4720640 | tf_op jit(solution)/shard_map/mk,mrh->krh/dot_general | solution.py:54
  422.3 3.5 fusion.8
  427.4 2.0 fusion.2
  429.3 59.9 %all-reduce.2 = (bf16[4,16,512]{2,0,1:T(4,128)(2,1)S(1)}, bf16[64,16,256]{2,0,1:T(8,128)(2,1)S(1)}) all-reduce(f32[4,16,512]{2,0,1:T(4,128)S(1)} %fusion.2, f32[64,16,256]{2,0,1:T(8,128)} %fusion.8), channel_id=1, replica_groups=mesh['grp'=8,'mem'=64] {'grp'}, use_global_device_ids=true, to_apply=%region_1.2 | all-reduce | flops 294912 | bytes 1769472 | tf_op jit(solution)/shard_map/psum | solution.py:104
  (72 shorter events, 32.6 us)
Async XLA Ops:
  7.2 105.5 %copy-start = (bf16[128,16,128]{2,1,0:T(8,128)(2,1)S(1)}, bf16[128,16,128]{2,1,0:T(8,128)(2,1)}, u32[]{:S(2)}) copy-start(bf16[128,16,128]{2,1,0:T(8,128)(2,1)} %param.11) | copy-start | bytes 1572868
  112.5 2.5 copy-start.8
  115.0 35.0 %all-to-all-start.1 = ((bf16[8,64,16,128]{3,1,2,0:T(8,128)(2,1)}), bf16[8,64,16,128]{3,1,2,0:T(8,128)(2,1)S(1)}, u32[]{:S(2)}, u32[]{:S(2)}) async-start(bf16[8,64,16,128]{3,1,2,0:T(8,128)(2,1)} %copy.94), calls=%async_computation.1 | async-start | bytes 4194304 | tf_op jit(solution)/shard_map/all_to_all | solution.py:79
  125.4 65.0 %copy-start.2 = (bf16[128,1024]{1,0:T(8,128)(2,1)S(1)}, bf16[128,1024]{1,0:T(8,128)(2,1)}, u32[]{:S(2)}) copy-start(bf16[128,1024]{1,0:T(8,128)(2,1)} %param.6) | copy-start | bytes 786436
  125.4 65.3 %copy-start.5 = (bf16[128,1024]{1,0:T(8,128)(2,1)S(1)}, bf16[128,1024]{1,0:T(8,128)(2,1)}, u32[]{:S(2)}) copy-start(bf16[128,1024]{1,0:T(8,128)(2,1)} %param.7) | copy-start | bytes 786436
  125.4 164.1 %all-gather.3.cloned.1.call-start = ((), (), s32[]{:S(2)}) async-start(), calls=%async_computation.6 | async-start | bytes 4259840 | tf_op jit(solution)/shard_map/all_gather | solution.py:71
  151.3 30.8 %all-to-all-start.2 = ((bf16[64,16,128]{2,1,0:T(8,128)(2,1)}), bf16[64,16,128]{2,1,0:T(8,128)(2,1)S(1)}, u32[]{:S(2)}, u32[]{:S(2)}) async-start(bf16[64,16,128]{2,1,0:T(8,128)(2,1)} %copy.96), calls=%async_computation.2 | async-start | bytes 524288 | tf_op jit(solution)/shard_map/all_to_all | solution.py:81
  182.1 37.1 %all-to-all-start = ((bf16[64,16,256]{2,1,0:T(8,128)(2,1)}), bf16[64,16,256]{2,1,0:T(8,128)(2,1)S(1)}, u32[]{:S(2)}, u32[]{:S(2)}) async-start(bf16[64,16,256]{2,1,0:T(8,128)(2,1)} %copy.91), calls=%async_computation | async-start | bytes 1048576 | tf_op jit(solution)/shard_map/all_to_all | solution.py:73
  219.1 10.5 %copy-start.6 = (bf16[64,16,256]{2,1,0:T(8,128)(2,1)}, bf16[64,16,256]{2,1,0:T(8,128)(2,1)S(1)}, u32[]{:S(2)}) copy-start(bf16[64,16,256]{2,1,0:T(8,128)(2,1)S(1)} %all-to-all-done) | copy-start | bytes 1572868
  219.1 45.3 %all-to-all-start.5 = ((f32[64,16,128]{2,1,0:T(8,128)}), f32[64,16,128]{2,1,0:T(8,128)}, u32[]{:S(2)}, u32[]{:S(2)}) async-start(f32[64,16,128]{2,1,0:T(8,128)} %bitcast.30), calls=%async_computation.5 | async-start | bytes 1048576 | tf_op jit(solution)/shard_map/all_to_all | solution.py:105
  229.4 42.9 %copy-start.9 = (s32[1,3]{1,0:T(1,128)S(1)}, s32[1,3]{1,0:T(1,128)}, u32[]{:S(2)}) copy-start(s32[1,3]{1,0:T(1,128)} %param.8) | copy-start | bytes 40
  264.4 59.5 %all-to-all-start.4 = ((f32[64,16,256]{2,1,0:T(8,128)}), f32[64,16,256]{2,1,0:T(8,128)}, u32[]{:S(2)}, u32[]{:S(2)}) async-start(f32[64,16,256]{2,1,0:T(8,128)} %bitcast.25), calls=%async_computation.4 | async-start | bytes 2097152 | tf_op jit(solution)/shard_map/all_to_all | solution.py:94
  290.8 1.0 copy-start.3
  323.9 103.5 %all-to-all-start.3 = ((f32[64,16,512]{2,1,0:T(8,128)}), f32[64,16,512]{2,1,0:T(8,128)S(1)}, u32[]{:S(2)}, u32[]{:S(2)}) async-start(f32[64,16,512]{2,1,0:T(8,128)} %bitcast.119), calls=%async_computation.3 | async-start | bytes 4194304 | tf_op jit(solution)/shard_map/all_to_all | solution.py:87
  337.5 1.9 copy-start.1
  341.1 18.3 %collective-permute-start = (f32[1,64,16,128]{3,2,1,0:T(8,128)}, f32[1,64,16,128]{3,2,1,0:T(8,128)}, u32[]{:S(2)}, u32[]{:S(2)}) collective-permute-start(f32[1,64,16,128]{3,2,1,0:T(8,128)} %get-tuple-element.32), channel_id=1, source_target_pairs={{0,64},{64,0},{128,192},{192,128},{256,320},{320,256},{384,448},{4... | collective-permute-start | bytes 1572872 | tf_op jit(solution)/shard_map/ppermute | solution.py:122
  344.8 19.5 %collective-permute-start.1 = (f32[1,64,16,128]{3,2,1,0:T(8,128)}, f32[1,64,16,128]{3,2,1,0:T(8,128)}, u32[]{:S(2)}, u32[]{:S(2)}) collective-permute-start(f32[1,64,16,128]{3,2,1,0:T(8,128)} %get-tuple-element.31), channel_id=1, source_target_pairs={{0,128},{64,192},{128,0},{192,64},{256,384},{320,448},{384,256},{4... | collective-permute-start | bytes 1572872 | tf_op jit(solution)/shard_map/ppermute | solution.py:122
  347.3 25.2 %collective-permute-start.2 = (f32[1,64,16,128]{3,2,1,0:T(8,128)}, f32[1,64,16,128]{3,2,1,0:T(8,128)S(1)}, u32[]{:S(2)}, u32[]{:S(2)}) collective-permute-start(f32[1,64,16,128]{3,2,1,0:T(8,128)} %get-tuple-element.30), channel_id=1, source_target_pairs={{0,192},{64,128},{128,64},{192,0},{256,448},{320,384},{384,320},{4... | collective-permute-start | bytes 1572872 | tf_op jit(solution)/shard_map/ppermute | solution.py:122
  352.2 31.6 %collective-permute-start.3 = (f32[1,64,16,128]{3,2,1,0:T(8,128)}, f32[1,64,16,128]{3,2,1,0:T(8,128)S(1)}, u32[]{:S(2)}, u32[]{:S(2)}) collective-permute-start(f32[1,64,16,128]{3,2,1,0:T(8,128)} %get-tuple-element.29), channel_id=1, source_target_pairs={{0,256},{64,320},{128,384},{192,448},{256,0},{320,64},{384,128},{4... | collective-permute-start | bytes 1572872 | tf_op jit(solution)/shard_map/ppermute | solution.py:122
  356.3 39.2 %collective-permute-start.4 = (f32[1,64,16,128]{3,2,1,0:T(8,128)}, f32[1,64,16,128]{3,2,1,0:T(8,128)S(1)}, u32[]{:S(2)}, u32[]{:S(2)}) collective-permute-start(f32[1,64,16,128]{3,2,1,0:T(8,128)} %get-tuple-element.28), channel_id=1, source_target_pairs={{0,320},{64,256},{128,448},{192,384},{256,64},{320,0},{384,192},{4... | collective-permute-start | bytes 1572872 | tf_op jit(solution)/shard_map/ppermute | solution.py:122
  359.4 39.3 %collective-permute-start.5 = (f32[1,64,16,128]{3,2,1,0:T(8,128)}, f32[1,64,16,128]{3,2,1,0:T(8,128)S(1)}, u32[]{:S(2)}, u32[]{:S(2)}) collective-permute-start(f32[1,64,16,128]{3,2,1,0:T(8,128)} %get-tuple-element.27), channel_id=1, source_target_pairs={{0,384},{64,448},{128,256},{192,320},{256,128},{320,192},{384,0},{... | collective-permute-start | bytes 1572872 | tf_op jit(solution)/shard_map/ppermute | solution.py:122
  364.3 46.0 %collective-permute-start.6 = (f32[1,64,16,128]{3,2,1,0:T(8,128)S(1)}, f32[1,64,16,128]{3,2,1,0:T(8,128)S(1)}, u32[]{:S(2)}, u32[]{:S(2)}) collective-permute-start(f32[1,64,16,128]{3,2,1,0:T(8,128)S(1)} %get-tuple-element.26), channel_id=1, source_target_pairs={{0,448},{64,384},{128,320},{192,256},{256,192},{320,128},{384,64},... | collective-permute-start | bytes 1572872 | tf_op jit(solution)/shard_map/ppermute | solution.py:122
  416.2 9.6 %copy-start.4 = (bf16[1024,512]{1,0:T(8,128)(2,1)S(1)}, bf16[1024,512]{1,0:T(8,128)(2,1)}, u32[]{:S(2)}) copy-start(bf16[1024,512]{1,0:T(8,128)(2,1)} %copy-done.3) | copy-start | bytes 3145732
  416.2 9.9 %copy-start.7 = (bf16[64,16,256]{2,1,0:T(8,128)(2,1)S(1)}, bf16[64,16,256]{2,1,0:T(8,128)(2,1)}, u32[]{:S(2)}) copy-start(bf16[64,16,256]{2,1,0:T(8,128)(2,1)} %copy-done.6) | copy-start | bytes 1572868
Sparse Core Ops, SparseCore 0:
  129.2 160.2 all-gather.2
